TPU v7x, 32 devices: a whole 2x2x4 slice. The times are simulated.
32 devices in a mesh: tp: 8 (over y, x, core), dp: 4 (over z).
Axes of the slice: x: 2, y: 2, z: 4, core: 2. Of those that a mesh axis runs over, the one named last changes fastest.
Arguments:
- block_input: bfloat16 [8192, 1024], P(('tp', 'dp')), may hold values from -6 to 6
- doc_starts: int32 [8192], P('tp'), may hold values from 0 to 1, as said below
- first_gain: bfloat16 [1024], replicated, may hold values from 0.099609375 to 1.8984375
- branch_weight: bfloat16 [1024, 1536], P(None, 'dp'), may hold values from -0.1875 to 0.1875
- lru_weight: bfloat16 [1024, 1536], P(None, 'dp'), may hold values from -0.1875 to 0.1875
- filter_taps: bfloat16 [4, 1536], P(None, 'dp'), may hold values from -3 to 3
- rate_gate: bfloat16 [6, 256, 256], replicated, may hold values from -0.375 to 0.375
- input_gate: bfloat16 [6, 256, 256], replicated, may hold values from -0.375 to 0.375
- rate_bias: bfloat16 [1536], replicated, may hold values from -3 to 3
- input_bias: bfloat16 [1536], replicated, may hold values from -3 to 3
- decay_logit: bfloat16 [1536], P('dp'), may hold values from 1.5 to 7.5
- out_weight: bfloat16 [1536, 1024], P('dp'), may hold values from -0.625 to 0.625
- second_gain: bfloat16 [1024], replicated, may hold values from 0.099609375 to 1.8984375
- feed_gate: bfloat16 [1024, 3072], P(None, 'dp'), may hold values from -0.1875 to 0.1875
- feed_up: bfloat16 [1024, 3072], P(None, 'dp'), may hold values from -0.1875 to 0.1875
- feed_down: bfloat16 [3072, 1024], P('dp'), may hold values from -0.21875 to 0.21875
- cotangent: bfloat16 [8192, 1024], P(('tp', 'dp')), may hold values from -12 to 12
Outputs:
- block_output: float32 [8192, 1024], P(('tp', 'dp'))
- input_grad: float32 [8192, 1024], P(('tp', 'dp'))
- first_gain_grad: float32 [1024], replicated
- branch_weight_grad: float32 [1024, 1536], P(None, 'dp')
- lru_weight_grad: float32 [1024, 1536], P(None, 'dp')
- filter_taps_grad: float32 [4, 1536], P(None, 'dp')
- rate_gate_grad: float32 [6, 256, 256], replicated
- input_gate_grad: float32 [6, 256, 256], replicated
- rate_bias_grad: float32 [1536], replicated
- input_bias_grad: float32 [1536], replicated
- decay_logit_grad: float32 [1536], P('dp')
- out_weight_grad: float32 [1536, 1024], P('dp')
- second_gain_grad: float32 [1024], replicated
- feed_gate_grad: float32 [1024, 3072], P(None, 'dp')
- feed_up_grad: float32 [1024, 3072], P(None, 'dp')
- feed_down_grad: float32 [3072, 1024], P('dp')
Inputs may be any that keep to these rules, and one draw needn't show every extreme that they name: `doc_starts`: tokens form rows of 1024; the first token of every row is 1, and elsewhere a 1 marks a document's first token.
All inputs are finite; a program needn't handle non-finite values.
Results may differ from a plain program's by a relative error of at most 0.018.
Values may be sent and summed in bfloat16 or wider, within the bound.
A program may use at most 192 MiB of HBM per device.

v0:
```python
import functools
import math

import jax
import jax.numpy as jnp
from jax import lax
from jax.experimental import pallas as pl
from jax.experimental.pallas import tpu as pltpu
from jax.sharding import PartitionSpec as P

EPS = 1e-06
DECAY_SCALE = 8.0
F32 = jnp.float32
BF16 = jnp.bfloat16
MESH = pl.DeviceIdType.MESH
VMEM = pltpu.VMEM
DMA = pltpu.SemaphoreType.DMA
NN = (((1,), (0,)), ((), ()))
NT = (((1,), (1,)), ((), ()))
TN = (((0,), (0,)), ((), ()))
HALO = 16
LANE = 128
GELU_A = math.sqrt(2.0 / math.pi)
GELU_B = 0.044715


def dot(left, right, form):
    return lax.dot_general(left, right, form, preferred_element_type=F32)


def sigmoid(v):
    return 1.0 / (1.0 + jnp.exp(-v))


def softplus(v):
    return jnp.maximum(v, 0.0) + jnp.log1p(jnp.exp(-jnp.abs(v)))


def gelu_both(v):
    square = v * v
    tanh = jnp.tanh(GELU_A * v * (1.0 + GELU_B * square))
    half = 0.5 * (1.0 + tanh)
    slope = half + 0.5 * v * (1.0 - tanh * tanh) * (GELU_A * (1.0 + 3.0 * GELU_B * square))
    return v * half, slope


def gelu_only(v):
    return v * (0.5 * (1.0 + jnp.tanh(GELU_A * v * (1.0 + GELU_B * v * v))))


class Place:
    def __init__(self, nz):
        self.nz = nz
        self.t = lax.axis_index("tp")
        self.z = lax.axis_index("dp")
        self.b = lax.rem(self.t, 8)
        self.core = lax.rem(self.t, 2)
        self.x = lax.rem(self.t // 2, 2)
        self.y = lax.rem(self.t // 4, 2)
        self.chip = self.b // 2

    def flip(self, r):
        t = self.t
        if r & 1:
            t = t + 2 - 4 * self.x
        if r & 2:
            t = t + 4 - 8 * self.y
        return t

    def chip_of(self, r):
        c = self.chip
        if r & 1:
            c = c + 1 - 2 * self.x
        if r & 2:
            c = c + 2 - 4 * self.y
        return c

    def plane(self, r):
        return (self.flip(r), self.z)

    def sibling(self):
        return (self.t + 1 - 2 * self.core, self.z)

    def along(self, d):
        return (self.t, lax.rem(self.z + d, self.nz))

    def z_from(self, d):
        return lax.rem(self.z + self.nz - d, self.nz)


def greet(peers):
    barrier = pltpu.get_barrier_semaphore()
    for peer in peers:
        pl.semaphore_signal(barrier, inc=1, device_id=peer, device_id_type=MESH)
    pl.semaphore_wait(barrier, len(peers))


def remote(src, dst, send, recv, peer):
    return pltpu.make_async_remote_copy(
        src_ref=src, dst_ref=dst, send_sem=send, recv_sem=recv, device_id=peer, device_id_type=MESH
    )


class Sends:
    def __init__(self):
        self.started = []

    def when(self, cond, action):
        if cond is None:
            action()
        else:
            pl.when(cond)(action)

    def go(self, make, cond=None):
        self.when(cond, lambda: make().start())
        self.started.append((cond, make))

    def start_if(self, cond, make):
        pl.when(cond)(lambda: make().start())
        self.started.append((None, make))

    def arrived(self, make, cond=None):
        self.when(cond, lambda: make().wait_recv())

    def sent(self, make):
        make().wait_send()
        self.started = [(cond, other) for cond, other in self.started if other is not make]

    def finish(self):
        for cond, make in self.started:
            self.when(cond, lambda: make().wait_send())


class PlaneGather:
    def __init__(self, me, out, piece, send, recv, at, cond=None, first=None, joined=None, ready=None):
        self.me, self.out, self.piece, self.cond, self.joined = me, out, piece, cond, joined
        self.send, self.recv, self.at, self.first, self.ready = send, recv, at, first, ready

    def copy(self, i, src, dst, peer):
        return remote(src, dst, self.send.at[self.at + (i,)], self.recv.at[self.at + (i,)], peer)

    def whole(self, i, r, peer, first=False):
        def make():
            place = self.piece(self.me.chip_of(r), self.me.core, None)
            return self.copy(i, self.first() if first and self.first else place, place, peer)
        return make

    def half(self, i, r, part, peer):
        def make():
            place = self.piece(self.me.chip_of(r), self.me.core, part)
            return self.copy(i, place, place, peer)
        return make

    def across(self, core):
        def make():
            place = self.joined(core)
            return self.copy(4, place, place, self.me.sibling())
        return make

    def begin(self):
        for i, r in ((0, 1), (1, 2)):
            self.out.go(self.whole(i, 0, self.me.plane(r), True), self.cond)
        if not self.joined:
            self.out.go(self.whole(4, 0, self.me.sibling(), True), self.cond)

    def relay(self):
        me = self.me
        for i, r, part in ((0, 1, 0), (1, 2, 1)):
            self.out.arrived(self.whole(i, r, me.plane(r)), self.cond)
            self.out.go(self.half(2 + i, r, part, me.plane(3 - r)), self.cond)
            if not self.joined:
                self.out.go(self.whole(4 + r, r, me.sibling()), self.cond)

    def far(self):
        for part in (0, 1):
            self.out.arrived(self.half(2 + part, 3, part, self.me.plane(2 - part)), self.cond)
        if self.joined:
            if self.ready:
                self.ready()
            self.out.go(self.across(self.me.core), self.cond)
        else:
            self.out.go(self.whole(7, 3, self.me.sibling()), self.cond)

    def end(self):
        me = self.me
        if self.joined:
            self.out.arrived(self.across(1 - me.core), self.cond)
            return
        for r in range(4):
            def make(r=r):
                place = self.piece(me.chip_of(r), 1 - me.core, None)
                return self.copy(4 + r, place, place, me.sibling())
            self.out.arrived(make, self.cond)


class PlaneSum:
    def __init__(self, me, out, block, recv, send_sem, recv_sem, at, source=None):
        self.me, self.out, self.block, self.got = me, out, block, recv
        self.send_sem, self.recv_sem, self.at = send_sem, recv_sem, at
        self.source = source or block
        self.near = {r: me.plane(r) for r in (1, 2)}

    def copy(self, i, src, peer):
        def make():
            return remote(
                src(), self.got(i), self.send_sem.at[self.at + (i,)], self.recv_sem.at[self.at + (i,)], peer
            )
        return make

    def put(self, i, cond=None):
        half = i // 2
        to = 3 if i % 2 else half + 1
        make = self.copy(i, lambda: self.source(to, half), self.near[half + 1])
        if cond is None:
            self.out.go(make)
        else:
            self.out.start_if(cond, make)

    def begin(self):
        for i in (1, 0, 3, 2):
            self.put(i)

    def wait(self, i):
        self.out.arrived(self.copy(i, lambda: self.got(i), self.me.plane(1)))

    def relay(self):
        for half, r in ((0, 2), (1, 1)):
            self.wait(2 * half + 1)
            mine = self.block(r, half)
            mine[...] = (mine[...].astype(F32) + self.got(2 * half + 1)[...].astype(F32)).astype(BF16)
            self.out.go(self.copy(4 + half, lambda r=r, half=half: self.block(r, half), self.me.plane(r)))

    def total(self, half):
        self.wait(2 * half)
        self.wait(4 + half)
        return self.got(2 * half)[...].astype(F32) + self.got(4 + half)[...].astype(F32)


def rows(i, size):
    return pl.ds(pl.multiple_of(i * size, size), size)


def rms(v, gain):
    return v * lax.rsqrt(jnp.mean(v * v, axis=-1, keepdims=True) + EPS) * gain


def head_lanes(h, width):
    return pl.ds(pl.multiple_of(h * width, width), width)


def tile_scan(a, b, row, back):
    for step in (1, 2, 4):
        if back:
            seen = row < 8 - step
            shift = 8 - step
        else:
            seen = row >= step
            shift = step
        b_before = jnp.where(seen, pltpu.roll(b, shift, 0), 0.0)
        a_before = jnp.where(seen, pltpu.roll(a, shift, 0), 1.0)
        b = b + a * b_before
        a = a * a_before
    return a, b


def forward_kernel(nz, heads, i_gain1, i_gain2, i_bias1, i_bias2, i_starts, i_taps, i_dlogit, i_x, i_rg, i_ig, cot, lw, bw, ow, fgate, fup, fdown,
                   o_wl, o_wb, o_wo, o_fb, o_lin, o_br, o_cv, o_rl, o_il, o_st, o_pr, o_y, o_wg, o_base, o_rgrad,
                   o_sin, o_mk, o_vec, o_g2g, o_vecs,
                   gain1, gain2, bias1, bias2, starts, taps_in, dlogit, sin, mk, vec, g2g, vecs,
                   x, rg, ig, base, rgrad, wl, wb, wo, f, cots, win, turned, fb, lin, br, cv, rl, il, st, pr, pst, ends, ms, hx,
                   res, s, h, lg, ug, ybuf, sbuf, srecv, sown, fc, acts, slopes, yp,
                   lsem, osem, zs, zr, ps, pr_sem, fcs, fcr, qs, qr, vs, vr, es, er, hs, hr, ss, sr, gs, gr, ks, kr, ys, yr):
    me = Place(nz)
    out, feeds = Sends(), Sends()
    tokens, model = x.shape
    lru = wl.shape[1]
    width = lru // heads
    own = lru // nz
    cols = f.shape[1]
    part = cols // (2 * nz)
    piece_rows = model // 8
    chunk = 256
    z = me.z

    window = pl.ds(pl.multiple_of((me.chip // 2) * (4 * part) + lax.rem(me.chip, 2) * LANE, LANE), 256)
    shift = 64 * lax.rem(me.chip, 2)
    mine = rows(z, own)
    local = [
        (fgate.at[:, window], win.at[0]),
        (fup.at[:, window], win.at[1]),
        (lw, wl.at[:, mine]),
        (bw, wb.at[:, mine]),
        (ow, wo.at[mine]),
        (fdown.at[rows(me.chip, 2 * part)], f.at[2, rows(z, 2 * part)]),
        (cot, cots.at[0]),
    ]
    local = [pltpu.make_async_copy(a, b, lsem.at[i]) for i, (a, b) in enumerate(local)]
    vectors = (
        (i_gain1, gain1), (i_gain2, gain2), (i_bias1, bias1), (i_bias2, bias2), (i_starts, starts), (i_taps, taps_in),
        (i_dlogit, dlogit),
    )
    vectors = [pltpu.make_async_copy(a, b, lsem.at[11 + i]) for i, (a, b) in enumerate(vectors)]
    more = [pltpu.make_async_copy(a, b, lsem.at[8 + i]) for i, (a, b) in enumerate(((i_x, x), (i_rg, rg), (i_ig, ig)))]
    for copy in vectors + more[:1] + local + more[1:]:
        copy.start()
    greet([me.along(d) for d in range(1, nz)] + [me.plane(r) for r in (1, 2, 3)] + [me.sibling()])
    for copy in vectors:
        copy.wait()
    vecs[...] = jnp.zeros(vecs.shape, F32)
    for i, v in enumerate((gain1, gain2, bias1, bias2, starts)):
        vecs[i:i + 1, 0:v.shape[0]] = v[...].astype(F32).reshape(1, v.shape[0])
    vecs[8:12, 0:own] = taps_in[...].astype(F32)
    vecs[12:13, 0:own] = dlogit[...].astype(F32).reshape(1, own)

    def vector(d, origin):
        def make():
            place = vec.at[:, rows(origin(), own)]
            return remote(vecs.at[8:16, 0:own], place, vs.at[d - 1], vr.at[d - 1], me.along(d))
        return make

    def halo():
        return remote(i_x.at[tokens - HALO:tokens], hx, hs.at[0], hr.at[0], me.along(1))

    out.go(halo)
    for d in range(1, nz):
        out.go(vector(d, lambda: z))

    mine_of = 4 * me.core + me.chip

    def slot(m, zz, b):
        if m < 2:
            return (wl, wb)[m].at[rows(b, piece_rows), rows(zz, own)]
        if m == 2:
            return wo.at[rows(zz, own), rows(b, LANE)]
        at = pl.ds(pl.multiple_of(zz * (2 * part) + me.core * part, part), part)
        return f.at[0:2, at] if m == 3 else f.at[2, at]

    def source(m):
        if m < 2:
            return (lw, bw)[m].at[rows(mine_of, piece_rows)]
        if m == 2:
            return ow.at[:, rows(mine_of, LANE)]
        if m == 3:
            return turned.at[:, pl.ds(pl.multiple_of(shift + me.core * part, 32), part)]
        return fdown.at[pl.ds(pl.multiple_of(me.chip * (2 * part) + me.core * part, part), part)]

    def origin(hop, right):
        return z - 1 - hop if right else z + 1 + hop

    def has(hop, right):
        return z - 1 - hop >= 0 if right else z + 1 + hop < nz

    def along(m, hop, right, from_me):
        def make():
            step = 1 if right else -1
            zz = z - step * hop if from_me else origin(hop, right)
            place = slot(m, zz, mine_of)
            src = source(m) if from_me and hop == 0 else place
            at = (m, hop, int(right))
            peer = (me.t, z + step if from_me else z)
            return remote(src, place, zs.at[at], zr.at[at], peer)
        return make

    def z_begin(m, hop=0):
        for right in (True, False):
            there = z + 1 < nz if right else z >= 1
            if hop:
                there = jnp.logical_and(there, has(hop - 1, right))
            (out if m < 3 else feeds).go(along(m, hop, right, True), there)

    gathers = {}
    for m in range(3):
        for hop in range(nz - 1):
            for right in (True, False):
                def place(chip, core, half, m=m, hop=hop, right=right):
                    zz, b = origin(hop, right), 4 * core + chip
                    if half is None:
                        return slot(m, zz, b)
                    if m < 2:
                        at = pl.ds(pl.multiple_of(b * piece_rows + half * (piece_rows // 2), piece_rows // 2), piece_rows // 2)
                        return (wl, wb)[m].at[at, rows(zz, own)]
                    at = pl.ds(pl.multiple_of(zz * own + half * (own // 2), own // 2), own // 2)
                    return wo.at[at, rows(b, LANE)]

                def joined(core, m=m, hop=hop, right=right):
                    zz = origin(hop, right)
                    if m < 2:
                        return (wl, wb)[m].at[rows(core, 4 * piece_rows), rows(zz, own)]
                    return wo.at[rows(zz, own), rows(core, 4 * LANE)]

                gathers[m, hop, right] = PlaneGather(
                    me, out, place, ps, pr_sem, (m, 2 * hop + int(right)), has(hop, right), joined=joined
                )

    def share(m, hop, right, from_me):
        def make():
            at = (m - 3, 2 * hop + int(right))
            place = slot(m, origin(hop, right), mine_of)
            if not from_me:
                other = pl.ds(pl.multiple_of(origin(hop, right) * (2 * part) + (1 - me.core) * part, part), part)
                place = f.at[0:2, other] if m == 3 else f.at[2, other]
            return remote(place, place, fcs.at[at], fcr.at[at], me.sibling())
        return make

    def z_step(m, hop):
        for right in (True, False):
            out.arrived(along(m, hop, right, False), has(hop, right))
        if hop + 1 < nz - 1:
            z_begin(m, hop + 1)
        for right in (True, False):
            if m < 3:
                gathers[m, hop, right].begin()
            else:
                feeds.go(share(m, hop, right, True), has(hop, right))

    def relay(m, hop):
        for right in (True, False):
            gathers[m, hop, right].relay()

    def far(m, hop):
        for right in (True, False):
            gathers[m, hop, right].far()

    def all_of(m):
        for hop in range(nz - 1):
            for right in (True, False):
                gathers[m, hop, right].end()

    half = tokens // 2

    def cot_whole(i, r, part_of):
        at = pl.ds(part_of * half, half)
        return lambda: remote(cot.at[at], cots.at[r, at], qs.at[2 * part_of + i], qr.at[2 * part_of + i], me.plane(r))

    def cot_part(part_of, r):
        at = pl.ds(part_of * half, half)
        return lambda: remote(cots.at[r, at], cots.at[3, at], qs.at[4 + part_of], qr.at[4 + part_of], me.plane(3 - r))

    def lanes(h):
        return head_lanes(h, width)

    def project(h, _):
        lin[h] = dot(fb[...], wl[:, lanes(h)], NN)
        taps = vec[0:4, lanes(h)]
        conv = taps[0:1] * lin[h, HALO:, :]
        for k in range(1, 4):
            conv = conv + taps[k:k + 1] * lin[h, HALO - k:HALO - k + tokens, :] * mk[:, k:k + 1]
        conv = conv.astype(BF16)
        cv[h] = conv
        rl[h] = (dot(conv, rg[h], NN) + vecs[2:3, lanes(h)]).astype(BF16)
        il[h] = (dot(conv, ig[h], NN) + vecs[3:4, lanes(h)]).astype(BF16)
        return 0

    row = lax.broadcasted_iota(jnp.int32, (8, width), 0)

    def scan_head(h, _):
        rate = softplus(-vec[4:5, lanes(h)]) * -DECAY_SCALE

        def tile(i, carried):
            state, factor = carried
            at = rows(i, 16)
            start = mk[at, 0:1]
            keep = 1.0 - start
            decay = jnp.exp(sigmoid(rl[h, at, :].astype(F32)) * rate)
            a = keep * decay
            scale = (start + keep * jnp.sqrt(1.0 - decay * decay)) * sigmoid(il[h, at, :].astype(F32))
            b = scale * cv[h, at, :].astype(F32)
            for t in range(2):
                cum, run = tile_scan(a[8 * t:8 * t + 8], b[8 * t:8 * t + 8], row, False)
                run = run + cum * state
                cum = cum * factor
                here = pl.ds(pl.multiple_of(i * 16 + 8 * t, 8), 8)
                st[h, here, :] = run
                pst[h, here, :] = cum
                state, factor = run[7:8], cum[7:8]
            return state, factor

        state, factor = lax.fori_loop(
            0, tokens // 16, tile, (jnp.zeros((1, width), F32), jnp.ones((1, width), F32)), unroll=4
        )
        ends[0, 0:1, lanes(h)] = state
        ends[0, 1:2, lanes(h)] = factor
        return 0

    def end_copy(d):
        return lambda: remote(ends.at[0], ends.at[d], es.at[d - 1], er.at[d - 1], me.along(d))

    def branch(h, _):
        br[h] = dot(fb[HALO:], wb[:, lanes(h)], NN)
        return 0

    def finish(h, _):
        state = st[h] + pst[h] * sin[:, lanes(h)]
        st[h] = state
        pr[:, lanes(h)] = (state * gelu_only(br[h])).astype(BF16)
        return 0

    def project_out(j, _):
        at = rows(j, chunk)
        res[:, at] = x[:, at].astype(F32) + dot(pr[...], wo[:, at], NN)
        return 0

    def second_copy(r):
        return lambda: remote(s.at[0:tokens], s.at[r * tokens:(r + 1) * tokens], ss.at[r - 1], sr.at[r - 1], me.plane(r))

    def second_part(part_of, r):
        at, to = (pl.ds(q * tokens + part_of * half, half) for q in (r, 3))
        return lambda: remote(s.at[at], s.at[to], ss.at[2 + part_of], sr.at[2 + part_of], me.plane(3 - r))

    saved = [
        (wl, o_wl), (wb, o_wb), (wo, o_wo), (fb, o_fb), (lin, o_lin), (br, o_br), (cv, o_cv), (rl, o_rl), (il, o_il),
        (st, o_st), (pr, o_pr), (sin, o_sin), (mk, o_mk), (vec, o_vec), (vecs, o_vecs),
    ]
    saved = [pltpu.make_async_copy(a, b, osem.at[i]) for i, (a, b) in enumerate(saved)]
    grad_sum = PlaneSum(
        me, out, lambda r, part: sbuf.at[r, pl.ds(part * half, half)], lambda i: srecv.at[i], gs, gr, ()
    )
    def feed_ahead(r):
        at = rows(r, tokens)

        def hidden_of(j, _):
            here = rows(j, chunk)
            second = s[at]
            act, slope = gelu_both(dot(second, f[0, here, :], NT))
            up = dot(second, f[1, here, :], NT)
            h[at, here] = (act * up).astype(BF16)
            acts[at, here] = act
            slopes[at, here] = up * slope
            return 0

        lax.fori_loop(0, cols // chunk, hidden_of, 0, unroll=3)

    def feed_back(r):
        at = rows(r, tokens)

        def grads_of(j, _):
            here = rows(j, chunk)
            hg = dot(cots[r], f[2, here, :], NT)
            lg[at, here] = (hg * slopes[at, here]).astype(BF16)
            ug[at, here] = (hg * acts[at, here]).astype(BF16)
            return 0

        lax.fori_loop(0, cols // chunk, grads_of, 0, unroll=3)

        def back_of(j, _):
            here = rows(j, chunk)
            value = dot(lg[at], f[0, :, here], NN) + dot(ug[at], f[1, :, here], NN)
            sbuf[r, :, here] = value.astype(BF16)
            return 0

        lax.fori_loop(0, model // chunk, back_of, 0, unroll=4)

    def near_ahead(r, _):
        feed_ahead(r)
        return 0

    def near_back(r, _):
        feed_back(r)
        grad_sum.put(0, r == 1)
        grad_sum.put(2, r == 2)
        return 0

    def far_ahead(i, _):
        feed_ahead(3 - 3 * i)
        return 0

    def far_back(i, _):
        feed_back(3 - 3 * i)
        for piece in (1, 3):
            grad_sum.put(piece, i == 0)
        return 0

    def out_of(j, _):
        here = rows(j, chunk)
        for r in range(4):
            value = dot(h[r * tokens:(r + 1) * tokens], f[2, :, here], NN)
            if r:
                ybuf[r - 1, :, here] = value.astype(BF16)
            else:
                base[:, here] = res[:, here] + value
        return 0

    def feed_half(zz, core):
        return pl.ds(pl.multiple_of(zz * (2 * part) + core * part, part), part)

    def core_copy(m, zz):
        at = (m, zz)
        return lambda: remote(f.at[m, feed_half(zz, 1 - me.core)], fc.at[m, zz], ks.at[at], kr.at[at], me.sibling())

    def feed_wgrad(m, left):
        def body(i, _):
            here = rows(i, chunk)
            right = jnp.concatenate([cots[r, :, here] for r in range(4)], axis=0) if m == 2 else s[:, here]
            for j in range(cols // chunk):
                f[m, pl.ds(j * chunk, chunk), here] = dot(left[:, j * chunk:(j + 1) * chunk], right, TN).astype(BF16)
            return 0

        lax.fori_loop(0, model // chunk, body, 0)
        for zz in range(nz):
            out.go(core_copy(m, zz))

    last = [
        pltpu.make_async_copy(a, b, osem.at[15 + i])
        for i, (a, b) in enumerate((
            (ybuf, o_y), (base, o_base), (fc, o_wg), (rgrad, o_rgrad), (g2g, o_g2g),
        ))
    ]
    y_sum = PlaneSum(
        me, out, lambda r, part_of: ybuf.at[r - 1, pl.ds(part_of * half, half)], lambda i: yp.at[i // 2], ys, yr, ()
    )
    own_turned = pltpu.make_async_copy(
        turned.at[:, pl.ds(pl.multiple_of(shift, 32), 2 * part)], f.at[0:2, rows(z, 2 * part)], lsem.at[7]
    )
    g1, g2 = vecs[0:1, 0:model], vecs[1:2, 0:model]
    start_row = vecs[4:5, 0:nz * tokens]

    z_begin(0)
    for i, r in ((0, 1), (1, 2)):
        out.go(cot_whole(i, r, 0))
    for d in range(1, nz):
        out.arrived(vector(d, lambda: me.z_from(d)))
    vec[:, mine] = vecs[8:16, 0:own]
    for copy in local[2:] + more[1:]:
        copy.wait()
    z_begin(1)
    out.arrived(halo)
    fb[0:HALO] = rms(hx[...].astype(F32), g1).astype(BF16)
    z_step(0, 0)
    z_begin(2)
    z_step(0, 1)
    z_step(1, 0)
    z_step(0, 2)
    z_step(1, 1)
    z_step(1, 2)
    length = nz * tokens
    lane = lax.broadcasted_iota(jnp.int32, (1, length), 1)
    keep_row = 1.0 - start_row
    valid = keep_row
    lines, later_lines = [start_row, valid], []
    for k in range(1, 4):
        if k > 1:
            valid = valid * jnp.where(lane >= k - 1, pltpu.roll(keep_row, k - 1, 1), 0.0)
            lines.append(valid)
        later_lines.append(jnp.where(lane < length - k, pltpu.roll(valid, length - k, 1), 0.0))
    ms[...] = jnp.concatenate(lines + later_lines + [jnp.zeros_like(start_row)], axis=0)
    mk[...] = jnp.concatenate([ms[:, rows(z, tokens)], jnp.zeros((LANE - 8, tokens), F32)], axis=0).T
    relay(0, 1)
    relay(0, 0)
    z_step(2, 0)
    relay(0, 2)
    for i in range(2):
        local[i].wait()
        turned[i] = win[i].T
    own_turned.start()
    more[0].wait()
    fb[HALO:] = rms(x[...].astype(F32), g1).astype(BF16)
    z_begin(3)
    far(0, 1)
    relay(1, 1)
    z_step(2, 1)
    z_begin(4)
    relay(1, 0)
    far(0, 2)
    relay(1, 2)
    far(0, 0)
    z_step(3, 0)
    for i, r in ((0, 1), (1, 2)):
        out.go(cot_whole(i, r, 1))
    all_of(0)
    lax.fori_loop(0, heads // 3, project, 0, unroll=2)
    z_step(2, 2)
    relay(2, 0)
    lax.fori_loop(heads // 3, heads, project, 0, unroll=2)
    far(1, 1)
    far(1, 0)
    relay(2, 1)
    far(1, 2)
    lax.fori_loop(0, 2 * heads // 3, scan_head, 0)
    lax.fori_loop(2 * heads // 3, heads, scan_head, 0)
    all_of(1)
    for d in range(1, nz):
        out.go(end_copy(d), z + d < nz)
    relay(2, 2)
    far(2, 0)
    for part_of in range(2):
        out.arrived(cot_whole(0, 1, part_of))
    out.go(cot_part(0, 1))
    z_step(4, 0)
    lax.fori_loop(0, heads, branch, 0, unroll=2)
    for part_of in range(2):
        out.arrived(cot_whole(1, 2, part_of))
    out.go(cot_part(1, 2))
    far(2, 1)
    far(2, 2)
    for d in range(1, nz):
        out.arrived(end_copy(d), z >= d)
    incoming = jnp.zeros((1, lru), F32)
    for d in range(nz - 1, 0, -1):
        end = ends[d, 0:1, :] + ends[d, 1:2, :] * incoming
        incoming = jnp.where(d <= z, end, incoming)
    sin[...] = incoming

    all_of(2)
    lax.fori_loop(0, heads, finish, 0, unroll=2)
    lax.fori_loop(0, model // chunk, project_out, 0)
    s[0:tokens] = rms(res[...], g2).astype(BF16)
    for r in (1, 2):
        out.go(second_copy(r))
    for copy in saved:
        copy.start()
    z_step(3, 1)
    z_step(4, 1)
    z_step(3, 2)
    for part_of, r in ((0, 2), (1, 1)):
        out.arrived(cot_part(part_of, r))
    out.arrived(second_copy(2))
    out.go(second_part(1, 2))
    out.arrived(second_copy(1))
    out.go(second_part(0, 1))
    for hop in range(nz - 1):
        for right in (True, False):
            out.arrived(share(3, hop, right, False), has(hop, right))
    own_turned.wait()
    lax.fori_loop(1, 3, near_ahead, 0)
    z_step(4, 2)
    for hop in range(nz - 1):
        for right in (True, False):
            out.arrived(share(4, hop, right, False), has(hop, right))
    lax.fori_loop(1, 3, near_back, 0)
    for part_of, near in ((0, 2), (1, 1)):
        out.arrived(second_part(part_of, near))
    lax.fori_loop(0, 2, far_ahead, 0)
    lax.fori_loop(0, 2, far_back, 0)
    feeds.finish()
    feed_wgrad(0, lg)
    lax.fori_loop(0, model // chunk, out_of, 0)
    last[0].start()
    y_sum.put(0)
    y_sum.put(2)
    grad_sum.relay()
    feed_wgrad(1, ug)
    feed_wgrad(2, h)
    for zz in range(nz):
        out.arrived(core_copy(1, zz))
        fc[1, zz] = (fc[1, zz].astype(F32) + f[1, feed_half(zz, me.core), :].astype(F32)).astype(BF16)
    for part_of in range(2):
        at = pl.ds(part_of * half, half)
        y_sum.wait(2 * part_of)
        base[at, :] = base[at, :] + yp[part_of].astype(F32)
    last[1].start()
    for part_of in range(2):
        at = pl.ds(part_of * half, half)
        sown[at, :] = sbuf[0, at, :].astype(F32) + grad_sum.total(part_of)
    sg = sown[...]
    value = res[...]
    q = sg * g2
    inv = lax.rsqrt(jnp.mean(value * value, axis=-1, keepdims=True) + EPS)
    pull = jnp.mean(q * value, axis=-1, keepdims=True)
    rgrad[...] = cots[0].astype(F32) + (inv * q - value * (inv * inv * inv * pull))
    g2g[...] = jnp.sum(sg * value * inv, axis=0, keepdims=True)
    last[3].start()
    last[4].start()
    for zz in range(nz):
        out.arrived(core_copy(2, zz))
        fc[2, zz] = (fc[2, zz].astype(F32) + f[2, feed_half(zz, me.core), :].astype(F32)).astype(BF16)
    for zz in range(nz):
        out.arrived(core_copy(0, zz))
        fc[0, zz] = (fc[0, zz].astype(F32) + f[0, feed_half(zz, me.core), :].astype(F32)).astype(BF16)
    last[2].start()
    for copy in saved + last:
        copy.wait()
    out.finish()


def forward(nz, gain1, gain2, bias1, bias2, starts, taps, dlogit, x, rg, ig, cot, lw, bw, ow, fgate, fup, fdown):
    tokens, model = x.shape
    heads, width = rg.shape[0], rg.shape[1]
    lru = heads * width
    cols = fgate.shape[1]
    k = nz - 1
    hbm = pl.BlockSpec(memory_space=pl.ANY)
    by_head = (heads, tokens, width)
    saved = [
        ((model, lru), BF16), ((model, lru), BF16), ((lru, model), BF16), ((HALO + tokens, model), BF16),
        ((heads, HALO + tokens, width), F32), (by_head, F32), (by_head, BF16), (by_head, BF16), (by_head, BF16),
        (by_head, F32), ((tokens, lru), BF16), ((3, tokens, model), BF16), ((3, nz, cols // (2 * nz), model), BF16),
        ((tokens, model), F32), ((tokens, model), F32),
    ]
    kept = [((1, lru), F32), ((tokens, LANE), F32), ((8, lru), F32), ((1, model), F32), ((16, lru), F32)]
    sems = []
    for shape in ((5, k, 2), (3, 2 * k, 5), (2, 2 * k), (6,), (k,), (k,), (1,), (4,), (6,), (3, nz), (3,)):
        sems += [DMA(shape)] * 2
    return pl.pallas_call(
        functools.partial(forward_kernel, nz, heads),
        out_shape=tuple(jax.ShapeDtypeStruct(*a) for a in saved + kept),
        in_specs=[hbm] * 17,
        out_specs=[hbm] * (len(saved) + len(kept)),
        scratch_shapes=[VMEM(v.shape, v.dtype) for v in (gain1, gain2, bias1, bias2, starts, taps, dlogit)]
        + [VMEM(*a) for a in kept]
        + [
            VMEM((tokens, model), BF16), VMEM((heads, width, width), BF16), VMEM((heads, width, width), BF16),
            VMEM((tokens, model), F32), VMEM((tokens, model), F32), VMEM((model, lru), BF16), VMEM((model, lru), BF16), VMEM((lru, model), BF16), VMEM((3, cols, model), BF16),
            VMEM((4, tokens, model), BF16), VMEM((2, model, 256), BF16), VMEM((2, 256, model), BF16),
            VMEM((HALO + tokens, model), BF16), VMEM((heads, HALO + tokens, width), F32), VMEM(by_head, F32),
            VMEM(by_head, BF16), VMEM(by_head, BF16), VMEM(by_head, BF16), VMEM(by_head, F32), VMEM((tokens, lru), BF16),
            VMEM(by_head, F32), VMEM((nz, 8, lru), F32), VMEM((8, nz * tokens), F32), VMEM((HALO, model), BF16),
            VMEM((tokens, model), F32), VMEM((4 * tokens, model), BF16), VMEM((4 * tokens, cols), BF16),
            VMEM((4 * tokens, cols), BF16), VMEM((4 * tokens, cols), BF16), VMEM((3, tokens, model), BF16),
            VMEM((4, tokens, model), BF16), VMEM((6, tokens // 2, model), BF16), VMEM((tokens, model), F32), VMEM((3, nz, cols // (2 * nz), model), BF16),
            VMEM((4 * tokens, cols), F32), VMEM((4 * tokens, cols), F32),
            VMEM((2, tokens // 2, model), BF16),
            DMA((18,)), DMA((len(saved) + len(kept),)),
        ] + sems,
        compiler_params=pltpu.CompilerParams(collective_id=0, has_side_effects=True, vmem_limit_bytes=62 * 2**20),
        name="forward_and_feed",
    )(gain1, gain2, bias1, bias2, starts, taps, dlogit, x, rg, ig, cot, lw, bw, ow, fgate, fup, fdown)


def backward_kernel(nz, heads, i_sin, i_mk, i_vec, i_vecs, i_g2g,
                    i_rg, i_ig, i_rgrad, i_x, i_wl, i_wb, i_wo, i_fb, i_lin, i_br, i_cv, i_rl, i_il, i_st, i_pr, i_base, i_y, i_ffg,
                    wa, fa, ga, o_bout, o_igrad, o_osm, o_osmz,
                    sin, mk, vec, vecs, g2g, osm, osmz, rg, ig, rgrad, bout, igrad, x, wl, wb, wo, fb, lin, br, cv, rl, il, st, pr, yk,
                    rgb, turned, fl, rlg, ilg, bg, lgr, ends, hal,
                    g, wc, wp, wz, fin, fc, fz, ffin, gt, gc, gp, gz, gfin, sm, smz, yp, inc,
                    lsem, osem, wcs, wcr, wps, wpr, wzs, wzr, was, war, fzs, fzr, fas, far,
                    gcs, gcr, gps, gpr, gzs, gzr, gys, gyr, gas, gar, yps, ypr, s1s, s1r, s2s, s2r,
                    es, er, hs, hr):
    me = Place(nz)
    out = Sends()
    core, other, chip, z = me.core, 1 - me.core, me.chip, me.z
    tokens, model = x.shape
    lru = wl.shape[1]
    width = lru // heads
    own = lru // nz
    block = model // 8
    half_rows = block // 2
    part = fc.shape[2]
    k = nz - 1

    loads = dict(
        rgrad=(i_rgrad, rgrad), g2g=(i_g2g, g2g), vec=(i_vec, vec), mk=(i_mk, mk), sin=(i_sin, sin), vecs=(i_vecs, vecs),
        fc=(i_ffg, fc), pr=(i_pr, pr), wo=(i_wo, wo), br=(i_br, br), st=(i_st, st),
        rl=(i_rl, rl), fb=(i_fb, fb), wb=(i_wb, wb), cv=(i_cv, cv), il=(i_il, il), lin=(i_lin, lin), wl=(i_wl, wl),
        y0=(i_y.at[1, 0:tokens // 2], yk.at[0]), y1=(i_y.at[0, tokens // 2:tokens], yk.at[1]),
        x=(i_x, x), base=(i_base, bout), rg=(i_rg, rg), ig=(i_ig, ig),
    )
    loads = {name: pltpu.make_async_copy(a, b, lsem.at[i]) for i, (name, (a, b)) in enumerate(loads.items())}
    for copy in loads.values():
        copy.start()

    def need(*names):
        for name in names:
            loads[name].wait()

    greet([me.along(d) for d in range(1, nz)] + [me.plane(r) for r in (1, 2, 3)] + [me.sibling()])


    def lanes(h):
        return head_lanes(h, width)

    def chain(i, right, from_me):
        def make():
            dest = nz - 1 - i if right else i
            peer = (me.t, z + (1 if right else -1) if from_me else z)
            at = (int(right), i)
            return remote(fc.at[:, dest], fz.at[at], fzs.at[at], fzr.at[at], peer)
        return make

    def chain_begin(i, right):
        out.go(chain(i, right, True), z == 0 if right else z == nz - 1)

    def chain_step(slot):
        for right in (True, False):
            i = slot - (z - 1 if right else nz - 2 - z)
            dest = nz - 1 - i if right else i
            here = jnp.logical_and(i >= 0, dest >= z if right else dest <= z)
            here = jnp.logical_and(here, z >= 1 if right else z <= nz - 2)
            onward = jnp.logical_and(here, dest != z)
            out.arrived(chain(i, right, False), here)

            @pl.when(here)
            def _(right=right, dest=dest, i=i):
                for m in range(3):
                    fc[m, dest] = (fc[m, dest].astype(F32) + fz[int(right), i, m].astype(F32)).astype(BF16)

            out.go(chain(i, right, True), onward)

    def feed_place(c, kk, half):
        at = pl.multiple_of((2 * c + kk) * part, part)
        if half is None:
            return fa.at[:, pl.ds(at, part)]
        return fa.at[:, pl.ds(pl.multiple_of(at + half * (part // 2), part // 2), part // 2)]

    feed_gather = PlaneGather(me, out, feed_place, fas, far, (), None, first=lambda: ffin)
    feed_own = pltpu.make_async_copy(ffin, feed_place(chip, core, None), osem.at[3])

    def feed_total():
        ffin[...] = fc[:, z]
        feed_gather.begin()
        feed_own.start()

    def y_half(r, half):
        return i_y.at[r - 1, pl.ds(half * (tokens // 2), tokens // 2)]

    y_sum = PlaneSum(me, out, lambda r, half: yk.at[half], lambda i: yp.at[{1: 0, 3: 1, 4: 2, 5: 3}[i]], yps, ypr, (), source=y_half)
    made = [pltpu.make_async_copy(a, b, osem.at[5 + i]) for i, (a, b) in enumerate(((bout, o_bout), (igrad, o_igrad), (osm, o_osm), (osmz, o_osmz)))]

    slot_of = {2: 0, 1: 1, 0: 0}

    def core_of(m):
        at = pl.ds(pl.multiple_of(other * (model // 2), model // 2), model // 2)
        return lambda: remote(g.at[slot_of[m], at], wc.at[m], wcs.at[m], wcr.at[m], me.sibling())

    core_copies = [core_of(m) for m in range(3)]

    def block_of(m, r, half=None):
        start = me.chip_of(r) * block
        if half is None:
            return wc.at[m, pl.ds(pl.multiple_of(start, block), block)]
        return wc.at[m, pl.ds(pl.multiple_of(start + half * half_rows, half_rows), half_rows)]

    sums = [
        PlaneSum(me, out, lambda r, half, m=m: block_of(m, r, half), lambda i, m=m: wp.at[m, i], wps, wpr, (m,))
        for m in range(3)
    ]

    def core_sum(m):
        out.arrived(core_copies[m])

        def add(c, _):
            at = rows(c, block)
            mine = pl.ds(pl.multiple_of(core * (model // 2) + c * block, block), block)
            wc[m, at, :] = (wc[m, at, :].astype(F32) + g[slot_of[m], mine, :].astype(F32)).astype(BF16)
            return 0

        lax.fori_loop(0, 4, add, 0)
        sums[m].begin()

    def z_copy(m, d):
        return lambda: remote(
            wc.at[m, rows(chip, block), rows(me.along(d)[1], own)], wz.at[m, d - 1], wzs.at[m, d - 1], wzr.at[m, d - 1], me.along(d)
        )

    def plane_total(m):
        for half in range(2):
            at = pl.ds(pl.multiple_of(chip * block + half * half_rows, half_rows), half_rows)
            wc[m, at, :] = (wc[m, at, :].astype(F32) + sums[m].total(half)).astype(BF16)
        for d in range(1, nz):
            out.go(z_copy(m, d))

    def weight_place(m):
        def place(c, kk, half):
            start = (4 * kk + c) * block
            if half is None:
                return wa.at[m, pl.ds(pl.multiple_of(start, block), block)]
            return wa.at[m, pl.ds(pl.multiple_of(start + half * half_rows, half_rows), half_rows)]
        return place

    own_copies = [pltpu.make_async_copy(fin.at[m], weight_place(m)(chip, core, None), osem.at[m]) for m in range(3)]
    gathers = [
        PlaneGather(
            me, out, weight_place(m), was, war, (m,), None, first=lambda m=m: fin.at[m],
            joined=lambda kk, m=m: wa.at[m, rows(kk, 4 * block)], ready=own_copies[m].wait,
        )
        for m in range(3)
    ]

    def z_total(m):
        for d in range(1, nz):
            out.arrived(z_copy(m, d))
        total = wc[m, rows(chip, block), rows(z, own)].astype(F32)
        for d in range(k):
            total = total + wz[m, d].astype(F32)
        fin[m] = total.astype(BF16)
        gathers[m].begin()
        own_copies[m].start()

    gate_half = gt.shape[0] // 2
    gate_block = gt.shape[0] // 8
    gate_part = gate_block // nz

    def gate_core():
        at = pl.ds(pl.multiple_of(other * gate_half, gate_half), gate_half)
        return remote(gt.at[at], gc, gcs.at[0], gcr.at[0], me.sibling())

    def gate_rows(r, half):
        return gc.at[pl.ds(pl.multiple_of(me.chip_of(r) * gate_block + half * (gate_block // 2), gate_block // 2), gate_block // 2)]

    gate_sum = PlaneSum(me, out, gate_rows, lambda i: gp.at[i], gps, gpr, ())

    def gate_core_sum():
        out.arrived(gate_core)
        mine = pl.ds(pl.multiple_of(core * gate_half, gate_half), gate_half)
        gc[...] = (gc[...].astype(F32) + gt[mine, :].astype(F32)).astype(BF16)
        gate_sum.begin()

    def gate_cut(i):
        return pl.ds(pl.multiple_of(chip * gate_block + i * gate_part, gate_part), gate_part)

    def gate_along(d):
        return lambda: remote(gc.at[gate_cut(me.along(d)[1])], gz.at[d - 1], gzs.at[d - 1], gzr.at[d - 1], me.along(d))

    def gate_back(d, origin):
        return lambda: remote(
            gfin.at[rows(origin(), gate_part)], gfin.at[rows(origin(), gate_part)], gys.at[d - 1], gyr.at[d - 1], me.along(d)
        )

    def gate_total():
        for half in range(2):
            at = pl.ds(pl.multiple_of(chip * gate_block + half * (gate_block // 2), gate_block // 2), gate_block // 2)
            gc[at, :] = (gc[at, :].astype(F32) + gate_sum.total(half)).astype(BF16)
        for d in range(1, nz):
            out.go(gate_along(d))

    def gate_z_total():
        for d in range(1, nz):
            out.arrived(gate_along(d))
        total = gc[gate_cut(z), :].astype(F32)
        for d in range(k):
            total = total + gz[d].astype(F32)
        gfin[rows(z, gate_part), :] = total.astype(BF16)
        for d in range(1, nz):
            out.go(gate_back(d, lambda: z))

    def gate_place(c, kk, half):
        start = (4 * kk + c) * gate_block
        if half is None:
            return ga.at[pl.ds(pl.multiple_of(start, gate_block), gate_block)]
        return ga.at[pl.ds(pl.multiple_of(start + half * (gate_block // 2), gate_block // 2), gate_block // 2)]

    gate_own = pltpu.make_async_copy(gfin, gate_place(chip, core, None), osem.at[4])
    gate_gather = PlaneGather(
        me, out, gate_place, gas, gar, (), None, first=lambda: gfin, joined=lambda kk: ga.at[rows(kk, 4 * gate_block)],
        ready=gate_own.wait,
    )

    def gate_spread():
        for d in range(1, nz):
            out.arrived(gate_back(d, lambda: me.z_from(d)))
        gate_gather.begin()
        gate_own.start()

    def small_copy(i):
        peer = (me.sibling(), me.plane(1), me.plane(2))[i]
        return lambda: remote(sm.at[2 * i], sm.at[2 * i + 1], s1s.at[i], s1r.at[i], peer)

    def small_step(i):
        out.arrived(small_copy(i))
        sm[2 * i + 2] = sm[2 * i] + sm[2 * i + 1]
        if i < 2:
            out.go(small_copy(i + 1))
        else:
            smz[z] = sm[6]
            for d in range(1, nz):
                out.go(small_along(d, lambda: z))

    def small_along(d, origin):
        return lambda: remote(sm.at[6], smz.at[origin()], s2s.at[d - 1], s2r.at[d - 1], me.along(d))


    small = sm.at[0]
    row = lax.broadcasted_iota(jnp.int32, (8, width), 0)

    def branch_back(h, _):
        pg = dot(rgb[...], wo[lanes(h), :], NT)
        act, slope = gelu_both(br[h])
        bg[:, lanes(h)] = (pg * st[h] * slope).astype(BF16)
        fl[h, 0:tokens] = pg * act
        return 0

    def scan_head(h, _):
        rate = softplus(-vec[4:5, lanes(h)]) * -DECAY_SCALE

        def tile(j, carried):
            later, factor = carried
            i = tokens // 16 - 1 - j
            at = rows(i, 16)
            keep = 1.0 - mk[at, 0:1]
            a = keep * jnp.exp(sigmoid(rl[h, at, :].astype(F32)) * rate)
            sgrad = fl[h, at, :]
            b = a * sgrad
            for t in (1, 0):
                cum, run = tile_scan(a[8 * t:8 * t + 8], b[8 * t:8 * t + 8], row, True)
                run = run + cum * later
                cum = cum * factor
                here = pl.ds(pl.multiple_of(i * 16 + 8 * t, 8), 8)
                last = row == 7
                fl[h, here, :] = sgrad[8 * t:8 * t + 8] + jnp.where(last, later, pltpu.roll(run, 7, 0))
                br[h, here, :] = jnp.where(last, factor, pltpu.roll(cum, 7, 0))
                later, factor = run[0:1], cum[0:1]
            return later, factor

        later, factor = lax.fori_loop(
            0, tokens // 16, tile, (jnp.zeros((1, width), F32), jnp.ones((1, width), F32)), unroll=4
        )
        ends[0, 0:1, lanes(h)] = later
        ends[0, 1:2, lanes(h)] = factor
        return 0

    def end_copy(d):
        return lambda: remote(ends.at[0], ends.at[d], es.at[d - 1], er.at[d - 1], me.along(nz - d))

    def wgrad(slot, right):
        def body(h, _):
            g[slot, :, lanes(h)] = dot(turned[...], right[:, lanes(h)], NN).astype(BF16)
            return 0

        lax.fori_loop(0, heads, body, 0)

    def terms(h, _):
        raw = vec[4:5, lanes(h)]
        soft = softplus(-raw)
        later = inc[:, lanes(h)]

        def tile(i, carried):
            before, decays, rates, inputs = carried
            at = rows(i, 16)
            start = mk[at, 0:1]
            keep = 1.0 - start
            flow = fl[h, at, :] + br[h, at, :] * later
            state = st[h, at, :]
            first = lax.broadcasted_iota(jnp.int32, (16, width), 0) == 0
            earlier = jnp.where(first, before, pltpu.roll(state, 1, 0))
            sig = sigmoid(rl[h, at, :].astype(F32))
            gate = sigmoid(il[h, at, :].astype(F32))
            decay = jnp.exp(sig * (soft * -DECAY_SCALE))
            root = jnp.sqrt(1.0 - decay * decay)
            level = start + keep * root
            conv = cv[h, at, :].astype(F32)
            to_scale = flow * conv
            to_decay = keep * (flow * earlier - to_scale * gate * (decay / root))
            to_power = to_decay * decay * sig
            rate_grad = (to_power * (1.0 - sig) * (soft * -DECAY_SCALE)).astype(BF16)
            input_grad = (to_scale * level * gate * (1.0 - gate)).astype(BF16)
            rlg[h, at, :] = rate_grad
            ilg[h, at, :] = input_grad
            fl[h, at, :] = flow * level * gate
            rates = rates + rate_grad.astype(F32)
            inputs = inputs + input_grad.astype(F32)
            return state[15:16], decays + to_power, rates, inputs

        zero = jnp.zeros((16, width), F32)
        _, decays, rates, inputs = lax.fori_loop(0, tokens // 16, tile, (sin[:, lanes(h)], zero, zero, zero), unroll=4)
        small[4:5, lanes(h)] = jnp.sum(decays, axis=0, keepdims=True) * (DECAY_SCALE * sigmoid(-raw))
        small[5:6, lanes(h)] = jnp.sum(rates, axis=0, keepdims=True)
        small[6:7, lanes(h)] = jnp.sum(inputs, axis=0, keepdims=True)
        rate_out, input_out = rlg[h], ilg[h]
        gt[rows(h, width), :] = dot(cv[h], rate_out, TN).astype(BF16)
        gt[rows(heads + h, width), :] = dot(cv[h], input_out, TN).astype(BF16)
        path = (dot(rate_out, rg[h], NT) + dot(input_out, ig[h], NT)).astype(BF16)
        fl[h, 0:tokens] = fl[h, 0:tokens] + path.astype(F32)
        hal[0, h] = fl[h, 0:8]
        return 0

    def halo():
        return remote(hal.at[0], hal.at[1], hs.at[0], hr.at[0], me.along(nz - 1))

    def first_back(left, right):
        def body(j, _):
            at = rows(j, 256)
            igrad[:, at] += dot(left[...], right[at, :], NT)
            return 0

        lax.fori_loop(0, model // 256, body, 0)

    def filter_back(h, _):
        taps = vec[0:4, lanes(h)]
        fl[h, tokens:tokens + 8] = hal[1, h]
        value = taps[0:1] * fl[h, 0:tokens]
        small[0:1, lanes(h)] = jnp.sum(fl[h, 0:tokens] * lin[h, HALO:], axis=0, keepdims=True)
        for t in range(1, 4):
            value = value + taps[t:t + 1] * (fl[h, t:t + tokens] * mk[:, 3 + t:4 + t])
            small[t:t + 1, lanes(h)] = jnp.sum(
                fl[h, 0:tokens] * (lin[h, HALO - t:HALO - t + tokens] * mk[:, t:t + 1]), axis=0, keepdims=True
            )
        lgr[:, lanes(h)] = value.astype(BF16)
        return 0

    y_sum.put(1)
    y_sum.put(3)
    need("g2g", "vec", "mk", "sin", "vecs", "fc")
    chain_begin(0, False)
    for i in range(k):
        chain_begin(i, True)
    small[...] = jnp.zeros(small.shape, F32)
    small[8:9, 0:model] = g2g[...]
    need("rgrad")
    rgb[...] = rgrad[...].astype(BF16)
    need("pr")
    turned[...] = rgb[...].T
    wgrad(0, pr)
    out.go(core_copies[2])
    need("wo", "br", "st")
    lax.fori_loop(0, heads, branch_back, 0)
    core_sum(2)
    need("rl")
    lax.fori_loop(0, heads // 2, scan_head, 0)
    need("y0", "y1")
    y_sum.relay()
    lax.fori_loop(heads // 2, heads, scan_head, 0)
    for d in range(1, nz):
        out.go(end_copy(d), z >= d)
    chain_begin(1, False)
    need("fb")
    turned[...] = fb[HALO:, :].T
    wgrad(1, bg)
    out.go(core_copies[1])
    chain_step(0)
    for d in range(1, nz):
        out.arrived(end_copy(d), z + d < nz)
    incoming = jnp.zeros((1, lru), F32)
    for d in range(nz - 1, 0, -1):
        end = ends[d, 0:1, :] + ends[d, 1:2, :] * incoming
        incoming = jnp.where(d + z < nz, end, incoming)
    inc[...] = incoming
    core_sum(1)
    sums[2].relay()
    need("cv", "il", "rg", "ig")
    lax.fori_loop(0, heads // 3, terms, 0)
    chain_begin(2, False)
    lax.fori_loop(heads // 3, heads, terms, 0)
    chain_step(1)
    out.go(gate_core)
    sums[1].relay()
    gate_core_sum()
    need("wb")
    igrad[...] = jnp.zeros(igrad.shape, F32)
    first_back(bg, wb)
    gate_sum.relay()
    out.go(halo)
    chain_step(2)
    feed_total()
    need("base")
    for half in range(2):
        at = pl.ds(half * (tokens // 2), tokens // 2)
        y_sum.wait(4 + half)
        bout[at, :] = bout[at, :] + yp[2 + half].astype(F32)
    made[0].start()
    plane_total(2)
    need("lin")
    out.arrived(halo)
    lax.fori_loop(0, heads, filter_back, 0)
    out.sent(core_copies[2])
    wgrad(0, lgr)
    out.go(core_copies[0])
    core_sum(0)
    gate_total()
    need("wl")
    first_back(lgr, wl)
    need("x")
    value = x[...].astype(F32)
    fgrad = igrad[...]
    q = fgrad * vecs[0:1, 0:model]
    inv = lax.rsqrt(jnp.mean(value * value, axis=-1, keepdims=True) + EPS)
    pull = jnp.mean(q * value, axis=-1, keepdims=True)
    small[7:8, 0:model] = jnp.sum(fgrad * value * inv, axis=0, keepdims=True)
    igrad[...] = rgrad[...] + (inv * q - value * (inv * inv * inv * pull))
    made[1].start()
    out.go(small_copy(0))
    gate_z_total()
    sums[0].relay()
    small_step(0)
    feed_gather.relay()
    plane_total(1)
    small_step(1)
    plane_total(0)
    gate_spread()
    z_total(1)
    z_total(2)
    small_step(2)
    gate_gather.relay()
    z_total(0)
    gathers[2].relay()
    feed_gather.far()
    gathers[1].relay()
    gate_gather.far()
    gathers[0].relay()
    gathers[2].far()
    for d in range(1, nz):
        out.arrived(small_along(d, lambda: me.z_from(d)))
    total = smz[0]
    for i in range(1, nz):
        total = total + smz[i]
    osm[...] = total
    osmz[...] = osm[:, rows(z, own)]
    made[2].start()
    made[3].start()
    gathers[1].far()
    gathers[0].far()
    for gathered in [feed_gather, gathers[2], gathers[1], gate_gather, gathers[0]]:
        gathered.end()
    for copy in [feed_own] + made:
        copy.wait()
    out.finish()


def backward(nz, sin, mk, vec, vecs, g2g, rg, ig, rgrad, x, wl, wb, wo, fb, lin, br, cv, rl, il, st, pr, base, y, ffg):
    tokens, model = x.shape
    heads, width = rg.shape[0], rg.shape[1]
    lru = heads * width
    own = lru // nz
    part = ffg.shape[2]
    k = nz - 1
    block = model // 8
    gate_rows = 2 * lru
    gate_block = gate_rows // 8
    hbm = pl.BlockSpec(memory_space=pl.ANY)
    by_head = (heads, tokens, width)
    half = tokens // 2
    sems = []
    for shape in (
        (3,), (3, 6), (3, k), (3, 8), (2, k), (8,),
        (1,), (6,), (k,), (k,), (8,), (6,), (3,), (k,), (k,), (1,),
    ):
        sems += [DMA(shape)] * 2
    return pl.pallas_call(
        functools.partial(backward_kernel, nz, heads),
        out_shape=(
            jax.ShapeDtypeStruct((3, model, own), BF16),
            jax.ShapeDtypeStruct((3, 8 * part, model), BF16),
            jax.ShapeDtypeStruct((gate_rows, width), BF16),
            jax.ShapeDtypeStruct((tokens, model), F32),
            jax.ShapeDtypeStruct((tokens, model), F32),
            jax.ShapeDtypeStruct((16, lru), F32),
            jax.ShapeDtypeStruct((16, own), F32),
        ),
        in_specs=[hbm] * 23,
        out_specs=[hbm] * 7,
        scratch_shapes=[
            VMEM(sin.shape, F32), VMEM(mk.shape, F32), VMEM(vec.shape, F32), VMEM(vecs.shape, F32), VMEM(g2g.shape, F32),
            VMEM((16, lru), F32), VMEM((16, own), F32),
            VMEM((heads, width, width), BF16), VMEM((heads, width, width), BF16), VMEM((tokens, model), F32),
            VMEM((tokens, model), F32), VMEM((tokens, model), F32),
            VMEM((tokens, model), BF16), VMEM((model, lru), BF16), VMEM((model, lru), BF16), VMEM((lru, model), BF16),
            VMEM((HALO + tokens, model), BF16), VMEM((heads, HALO + tokens, width), F32), VMEM(by_head, F32),
            VMEM(by_head, BF16), VMEM(by_head, BF16), VMEM(by_head, BF16), VMEM(by_head, F32), VMEM((tokens, lru), BF16),
            VMEM((2, half, model), BF16),
            VMEM((tokens, model), BF16), VMEM((model, tokens), BF16), VMEM((heads, tokens + 8, width), F32),
            VMEM(by_head, BF16), VMEM(by_head, BF16), VMEM((tokens, lru), BF16), VMEM((tokens, lru), BF16),
            VMEM((nz, 8, lru), F32), VMEM((2, heads, 8, width), F32),
            VMEM((2, model, lru), BF16), VMEM((3, model // 2, lru), BF16), VMEM((3, 6, block // 2, lru), BF16),
            VMEM((3, k, block, own), BF16), VMEM((3, block, own), BF16),
            VMEM((3, nz, part, model), BF16), VMEM((2, k, 3, part, model), BF16), VMEM((3, part, model), BF16),
            VMEM((gate_rows, width), BF16), VMEM((gate_rows // 2, width), BF16), VMEM((6, gate_block // 2, width), BF16),
            VMEM((k, gate_block // nz, width), BF16), VMEM((gate_block, width), BF16),
            VMEM((7, 16, lru), F32), VMEM((nz, 16, lru), F32), VMEM((4, half, model), BF16), VMEM((1, lru), F32),
            DMA((25,)), DMA((9,)),
        ] + sems,
        compiler_params=pltpu.CompilerParams(collective_id=1, has_side_effects=True, vmem_limit_bytes=62 * 2**20),
        name="backward_and_sums",
    )(sin, mk, vec, vecs, g2g, rg, ig, rgrad, x, wl, wb, wo, fb, lin, br, cv, rl, il, st, pr, base, y, ffg)


def results_kernel(wa, fa, ga, gb, bout, igrad, osm, osmz,
                   o_out, o_in, o_g1, o_branch, o_lru, o_taps, o_rate, o_input, o_rb, o_ib, o_decay, o_ow, o_g2, o_gate, o_up, o_down):
    model = bout.shape[1]

    @pl.when(pl.program_id(0) == 0)
    def _():
        o_out[...] = bout[...]
        o_in[...] = igrad[...]
        o_taps[...] = osmz[0:4, :]
        o_decay[...] = osmz[4, :]
        o_rb[...] = osm[5, :]
        o_ib[...] = osm[6, :]
        o_g1[...] = osm[7, 0:model]
        o_g2[...] = osm[8, 0:model]

    o_lru[...] = wa[0].astype(F32)
    o_branch[...] = wa[1].astype(F32)
    o_ow[...] = wa[2].T.astype(F32)
    o_rate[...] = ga[...].astype(F32)
    o_input[...] = gb[...].astype(F32)
    o_gate[...] = fa[0].T.astype(F32)
    o_up[...] = fa[1].T.astype(F32)
    o_down[...] = fa[2].astype(F32)


def results(wa, fa, ga, bout, igrad, osm, osmz):
    steps = 3
    model, own = wa.shape[1:]
    cols = fa.shape[1]
    gate_rows, width = ga.shape[0] // 2, ga.shape[1]
    lru = osm.shape[1]
    tokens = bout.shape[0]

    def whole(shape):
        return pl.BlockSpec(shape, lambda i: (0,) * len(shape))

    across = pl.BlockSpec((model, own // steps), lambda i: (0, i))
    feed_across = pl.BlockSpec((model, cols // steps), lambda i: (0, i))
    outs = [
        ((tokens, model), whole((tokens, model))), ((tokens, model), whole((tokens, model))), ((model,), whole((model,))),
        ((model, own), across), ((model, own), across), ((4, own), whole((4, own))),
        ((gate_rows, width), pl.BlockSpec((gate_rows // steps, width), lambda i: (i, 0))),
        ((gate_rows, width), pl.BlockSpec((gate_rows // steps, width), lambda i: (i, 0))),
        ((lru,), whole((lru,))), ((lru,), whole((lru,))), ((own,), whole((own,))),
        ((own, model), pl.BlockSpec((own // steps, model), lambda i: (i, 0))), ((model,), whole((model,))),
        ((model, cols), feed_across), ((model, cols), feed_across),
        ((cols, model), pl.BlockSpec((cols // steps, model), lambda i: (i, 0))),
    ]
    return pl.pallas_call(
        results_kernel,
        grid=(steps,),
        out_shape=tuple(jax.ShapeDtypeStruct(shape, F32) for shape, _ in outs),
        in_specs=[
            pl.BlockSpec((3, model, own // steps), lambda i: (0, 0, i)),
            pl.BlockSpec((3, cols // steps, model), lambda i: (0, i, 0)),
            pl.BlockSpec((gate_rows // steps, width), lambda i: (i, 0)),
            pl.BlockSpec((gate_rows // steps, width), lambda i: (i + steps, 0)),
            whole((tokens, model)), whole((tokens, model)), whole((16, lru)), whole((16, own)),
        ],
        out_specs=tuple(spec for _, spec in outs),
        compiler_params=pltpu.CompilerParams(vmem_limit_bytes=62 * 2**20),
        name="results",
    )(wa, fa, ga, ga, bout, igrad, osm, osmz)


def local(
    nz,
    groups,
    block_input,
    doc_starts,
    first_gain,
    branch_weight,
    lru_weight,
    filter_taps,
    rate_gate,
    input_gate,
    rate_bias,
    input_bias,
    decay_logit,
    out_weight,
    second_gain,
    feed_gate,
    feed_up,
    feed_down,
    cotangent,
):
    model = block_input.shape[1]
    heads, width = rate_gate.shape[:2]
    lru = heads * width

    (wl, wb, wo, fb, lin, br, cv, rl, il, st, pr, y, ffg, base, rgrad, sin, mk, vec, g2g, vecs) = forward(
        nz, first_gain, second_gain, rate_bias, input_bias, doc_starts, filter_taps, decay_logit, block_input, rate_gate,
        input_gate, cotangent, lru_weight, branch_weight, out_weight,
        feed_gate, feed_up, feed_down,
    )
    sums = backward(
        nz, sin, mk, vec, vecs, g2g, rate_gate, input_gate, rgrad, block_input, wl, wb, wo, fb, lin, br, cv, rl, il, st, pr,
        base, y, ffg,
    )
    made = results(*sums)
    block_output, input_grad, *summed = made
    if groups > 1:
        same = [[8 * g + b for g in range(groups)] for b in range(8)]
        summed = lax.psum(tuple(summed), "tp", axis_index_groups=same)
    g1, branch, lru_grad, taps, rate, inputs, rb, ib, decay, ow, g2, gate, up, down = summed
    rate, inputs = rate.reshape(heads, width, width), inputs.reshape(heads, width, width)
    return (
        block_output, input_grad, g1, branch, lru_grad, taps, rate, inputs, rb, ib, decay, ow, g2,
        gate, up, down,
    )


def solution(mesh):
    by_rows = P(("tp", "dp"), None)
    by_cols = P(None, "dp")
    split = P("dp", None)
    return jax.shard_map(
        functools.partial(local, mesh.shape["dp"], mesh.shape["tp"] // 8),
        mesh=mesh,
        in_specs=(
            by_rows, P("tp"), P(), by_cols, by_cols, by_cols, P(), P(), P(), P(), P("dp"), split, P(), by_cols, by_cols,
            split, by_rows,
        ),
        out_specs=(
            by_rows, by_rows, P(), by_cols, by_cols, by_cols, P(), P(), P(), P(), P("dp"), split, P(), by_cols, by_cols,
            split,
        ),
        check_vma=False,
    )
```

profile of v0, /device:TPU:1, one launch (start us, length us, event | category | flops | bytes accessed | tf_op | source)
XLA Modules:
  0.0 221.6 jit_solution(14458248428112297083)
XLA Ops:
  0.7 103.3 %forward_and_feed.1 = (bf16[1024,1536]{1,0:T(8,128)(2,1)}, bf16[1024,1536]{1,0:T(8,128)(2,1)}, bf16[1536,1024]{1,0:T(8,128)(2,1)}, bf16[272,1024]{1,0:T(8,128)(2...) custom-call(bf16[1024]{0:T(1024)(128)(2,1)} %i_gain1.1, ...), custom_call_target="tpu_custom_call" | custom-call | tf_op jit(solution)/shard_map/forward_and_feed/pallas_call | solution.py:793
  103.9 107.3 %backward_and_sums.1 = (bf16[3,1024,384]{2,1,0:T(8,128)(2,1)}, bf16[3,768,1024]{2,1,0:T(8,128)(2,1)}, bf16[3072,256]{1,0:T(8,128)(2,1)}, f32[256,1024]{1,0:T(8,1...) custom-call(f32[1,1536]{1,0:T(1,128)} %get-tuple-element.59.i_sin, ...), custom_call_target="tpu_custom_call" | custom-call | tf_op jit(solution)/shard_map/backward_and_sums/pallas_call | solution.py:1316
  211.3 10.2 %results.1 = (f32[256,1024]{1,0:T(8,128)}, f32[256,1024]{1,0:T(8,128)}, f32[1024]{0:T(1024)}, f32[1024,384]{1,0:T(8,128)}, f32[1024,384]{1,0:T(8,128)}, /*index=...) custom-call(bf16[3,1024,384]{2,1,0:T(8,128)(2,1)} %get-tuple-element, ...), custom_call_target="tpu_custom_call" | custom-call | tf_op jit(solution)/shard_map/results/pallas_call | solution.py:1402
where the time goes:
time: 222 us
  Pallas kernels  221 us (100%)
    pallas_call x1, Pallas kernels, backward(): pl.pallas_call(functools.partial(backward_kernel, nz, heads), out_shape=(...  107 us
    pallas_call x1, Pallas kernels, forward(): pl.pallas_call(functools.partial(forward_kernel, nz, heads), out_shape=tu...  103 us
    pallas_call x1, Pallas kernels, results(): pl.pallas_call(results_kernel, grid=(steps,), out_shape=tuple((jax.ShapeD...  10.2 us

commit v1 on v0

--- a/solution.py
+++ b/solution.py
@@ -702,7 +702,7 @@
 
     all_of(2)
     lax.fori_loop(0, heads, finish, 0, unroll=2)
-    lax.fori_loop(0, model // chunk, project_out, 0)
+    lax.fori_loop(0, model // chunk, project_out, 0, unroll=4)
     s[0:tokens] = rms(res[...], g2).astype(BF16)
     for r in (1, 2):
         out.go(second_copy(r))
@@ -733,7 +733,7 @@
     lax.fori_loop(0, 2, far_back, 0)
     feeds.finish()
     feed_wgrad(0, lg)
-    lax.fori_loop(0, model // chunk, out_of, 0)
+    lax.fori_loop(0, model // chunk, out_of, 0, unroll=2)
     last[0].start()
     y_sum.put(0)
     y_sum.put(2)
@@ -1183,7 +1183,8 @@
     for i in range(k):
         chain_begin(i, True)
     small[...] = jnp.zeros(small.shape, F32)
-    small[8:9, 0:model] = g2g[...]
+    for i in range(8):
+        small[i:i + 1, lru:lru + LANE] = g2g[:, i * LANE:(i + 1) * LANE]
     need("rgrad")
     rgb[...] = rgrad[...].astype(BF16)
     need("pr")
@@ -1191,7 +1192,7 @@
     wgrad(0, pr)
     out.go(core_copies[2])
     need("wo", "br", "st")
-    lax.fori_loop(0, heads, branch_back, 0)
+    lax.fori_loop(0, heads, branch_back, 0, unroll=3)
     core_sum(2)
     need("rl")
     lax.fori_loop(0, heads // 2, scan_head, 0)
@@ -1321,14 +1322,14 @@
             jax.ShapeDtypeStruct((gate_rows, width), BF16),
             jax.ShapeDtypeStruct((tokens, model), F32),
             jax.ShapeDtypeStruct((tokens, model), F32),
-            jax.ShapeDtypeStruct((16, lru), F32),
-            jax.ShapeDtypeStruct((16, own), F32),
+            jax.ShapeDtypeStruct((8, lru + LANE), F32),
+            jax.ShapeDtypeStruct((8, own), F32),
         ),
         in_specs=[hbm] * 23,
         out_specs=[hbm] * 7,
         scratch_shapes=[
             VMEM(sin.shape, F32), VMEM(mk.shape, F32), VMEM(vec.shape, F32), VMEM(vecs.shape, F32), VMEM(g2g.shape, F32),
-            VMEM((16, lru), F32), VMEM((16, own), F32),
+            VMEM((8, lru + LANE), F32), VMEM((8, own), F32),
             VMEM((heads, width, width), BF16), VMEM((heads, width, width), BF16), VMEM((tokens, model), F32),
             VMEM((tokens, model), F32), VMEM((tokens, model), F32),
             VMEM((tokens, model), BF16), VMEM((model, lru), BF16), VMEM((model, lru), BF16), VMEM((lru, model), BF16),
@@ -1343,7 +1344,7 @@
             VMEM((3, nz, part, model), BF16), VMEM((2, k, 3, part, model), BF16), VMEM((3, part, model), BF16),
             VMEM((gate_rows, width), BF16), VMEM((gate_rows // 2, width), BF16), VMEM((6, gate_block // 2, width), BF16),
             VMEM((k, gate_block // nz, width), BF16), VMEM((gate_block, width), BF16),
-            VMEM((7, 16, lru), F32), VMEM((nz, 16, lru), F32), VMEM((4, half, model), BF16), VMEM((1, lru), F32),
+            VMEM((7, 8, lru + LANE), F32), VMEM((nz, 8, lru + LANE), F32), VMEM((4, half, model), BF16), VMEM((1, lru), F32),
             DMA((25,)), DMA((9,)),
         ] + sems,
         compiler_params=pltpu.CompilerParams(collective_id=1, has_side_effects=True, vmem_limit_bytes=62 * 2**20),
@@ -1351,21 +1352,23 @@
     )(sin, mk, vec, vecs, g2g, rg, ig, rgrad, x, wl, wb, wo, fb, lin, br, cv, rl, il, st, pr, base, y, ffg)
 
 
-def results_kernel(wa, fa, ga, gb, bout, igrad, osm, osmz,
+def results_kernel(wa, fa, fd, ga, gb, bout, igrad, osm, osmz,
                    o_out, o_in, o_g1, o_branch, o_lru, o_taps, o_rate, o_input, o_rb, o_ib, o_decay, o_ow, o_g2, o_gate, o_up, o_down):
     model = bout.shape[1]
 
     @pl.when(pl.program_id(0) == 0)
     def _():
-        o_out[...] = bout[...]
-        o_in[...] = igrad[...]
         o_taps[...] = osmz[0:4, :]
         o_decay[...] = osmz[4, :]
-        o_rb[...] = osm[5, :]
-        o_ib[...] = osm[6, :]
+        lru = o_rb.shape[0]
+        o_rb[...] = osm[5, 0:lru]
+        o_ib[...] = osm[6, 0:lru]
         o_g1[...] = osm[7, 0:model]
-        o_g2[...] = osm[8, 0:model]
-
+        for i in range(8):
+            o_g2[i * LANE:(i + 1) * LANE] = osm[i, lru:lru + LANE]
+
+    o_out[...] = bout[...]
+    o_in[...] = igrad[...]
     o_lru[...] = wa[0].astype(F32)
     o_branch[...] = wa[1].astype(F32)
     o_ow[...] = wa[2].T.astype(F32)
@@ -1373,47 +1376,47 @@
     o_input[...] = gb[...].astype(F32)
     o_gate[...] = fa[0].T.astype(F32)
     o_up[...] = fa[1].T.astype(F32)
-    o_down[...] = fa[2].astype(F32)
+    o_down[...] = fd[0].astype(F32)
 
 
 def results(wa, fa, ga, bout, igrad, osm, osmz):
-    steps = 3
+    steps = 2
     model, own = wa.shape[1:]
     cols = fa.shape[1]
     gate_rows, width = ga.shape[0] // 2, ga.shape[1]
-    lru = osm.shape[1]
+    lru = osm.shape[1] - LANE
     tokens = bout.shape[0]
 
     def whole(shape):
         return pl.BlockSpec(shape, lambda i: (0,) * len(shape))
 
-    across = pl.BlockSpec((model, own // steps), lambda i: (0, i))
-    feed_across = pl.BlockSpec((model, cols // steps), lambda i: (0, i))
+    def down(count, lanes):
+        return pl.BlockSpec((count // steps, lanes), lambda i: (i, 0))
+
     outs = [
-        ((tokens, model), whole((tokens, model))), ((tokens, model), whole((tokens, model))), ((model,), whole((model,))),
-        ((model, own), across), ((model, own), across), ((4, own), whole((4, own))),
-        ((gate_rows, width), pl.BlockSpec((gate_rows // steps, width), lambda i: (i, 0))),
-        ((gate_rows, width), pl.BlockSpec((gate_rows // steps, width), lambda i: (i, 0))),
+        ((tokens, model), down(tokens, model)), ((tokens, model), down(tokens, model)), ((model,), whole((model,))),
+        ((model, own), down(model, own)), ((model, own), down(model, own)), ((4, own), whole((4, own))),
+        ((gate_rows, width), down(gate_rows, width)), ((gate_rows, width), down(gate_rows, width)),
         ((lru,), whole((lru,))), ((lru,), whole((lru,))), ((own,), whole((own,))),
-        ((own, model), pl.BlockSpec((own // steps, model), lambda i: (i, 0))), ((model,), whole((model,))),
-        ((model, cols), feed_across), ((model, cols), feed_across),
-        ((cols, model), pl.BlockSpec((cols // steps, model), lambda i: (i, 0))),
+        ((own, model), pl.BlockSpec((own, model // steps), lambda i: (0, i))), ((model,), whole((model,))),
+        ((model, cols), down(model, cols)), ((model, cols), down(model, cols)), ((cols, model), down(cols, model)),
     ]
     return pl.pallas_call(
         results_kernel,
         grid=(steps,),
         out_shape=tuple(jax.ShapeDtypeStruct(shape, F32) for shape, _ in outs),
         in_specs=[
-            pl.BlockSpec((3, model, own // steps), lambda i: (0, 0, i)),
-            pl.BlockSpec((3, cols // steps, model), lambda i: (0, i, 0)),
-            pl.BlockSpec((gate_rows // steps, width), lambda i: (i, 0)),
+            pl.BlockSpec((3, model // steps, own), lambda i: (0, i, 0)),
+            pl.BlockSpec((2, cols, model // steps), lambda i: (0, 0, i)),
+            pl.BlockSpec((1, cols // steps, model), lambda i: (2, i, 0)),
+            down(gate_rows, width),
             pl.BlockSpec((gate_rows // steps, width), lambda i: (i + steps, 0)),
-            whole((tokens, model)), whole((tokens, model)), whole((16, lru)), whole((16, own)),
+            down(tokens, model), down(tokens, model), whole(osm.shape), whole(osmz.shape),
         ],
         out_specs=tuple(spec for _, spec in outs),
         compiler_params=pltpu.CompilerParams(vmem_limit_bytes=62 * 2**20),
         name="results",
-    )(wa, fa, ga, ga, bout, igrad, osm, osmz)
+    )(wa, fa, fa, ga, ga, bout, igrad, osm, osmz)
 
 
 def local(

time: 222 us -> 219 us (0.986)
  Pallas kernels: 221 us -> 218 us
where the time goes in v1:
time: 219 us
  Pallas kernels  218 us (100%)
    pallas_call x1, Pallas kernels, backward(): pl.pallas_call(functools.partial(backward_kernel, nz, heads), out_shape=(...  106 us
    pallas_call x1, Pallas kernels, forward(): pl.pallas_call(functools.partial(forward_kernel, nz, heads), out_shape=tu...  102 us
    pallas_call x1, Pallas kernels, results(): pl.pallas_call(results_kernel, grid=(steps,), out_shape=tuple((jax.ShapeD...  9.76 us

profile of v1, /device:TPU:1, one launch (start us, length us, event | category | flops | bytes accessed | tf_op | source)
XLA Modules:
  0.0 219.3 jit_solution(2906355239149671457)
XLA Ops:
  0.7 102.4 %forward_and_feed.1 = (bf16[1024,1536]{1,0:T(8,128)(2,1)}, bf16[1024,1536]{1,0:T(8,128)(2,1)}, bf16[1536,1024]{1,0:T(8,128)(2,1)}, bf16[272,1024]{1,0:T(8,128)(2...) custom-call(bf16[1024]{0:T(1024)(128)(2,1)} %i_gain1.1, ...), custom_call_target="tpu_custom_call" | custom-call | tf_op jit(solution)/shard_map/forward_and_feed/pallas_call | solution.py:793
  103.0 106.3 %backward_and_sums.1 = (bf16[3,1024,384]{2,1,0:T(8,128)(2,1)}, bf16[3,768,1024]{2,1,0:T(8,128)(2,1)}, bf16[3072,256]{1,0:T(8,128)(2,1)}, f32[256,1024]{1,0:T(8,1...) custom-call(f32[1,1536]{1,0:T(1,128)} %get-tuple-element.59.i_sin, ...), custom_call_target="tpu_custom_call" | custom-call | tf_op jit(solution)/shard_map/backward_and_sums/pallas_call | solution.py:1317
  209.4 9.8 %results.1 = (f32[256,1024]{1,0:T(8,128)}, f32[256,1024]{1,0:T(8,128)}, f32[1024]{0:T(1024)}, f32[1024,384]{1,0:T(8,128)}, f32[1024,384]{1,0:T(8,128)}, /*index=...) custom-call(bf16[3,1024,384]{2,1,0:T(8,128)(2,1)} %get-tuple-element, ...), custom_call_target="tpu_custom_call" | custom-call | tf_op jit(solution)/shard_map/results/pallas_call | solution.py:1404
